TPU v7x, 128 devices: a whole 4x4x4 slice. The times are simulated.
128 devices in a mesh: hst: 16 (over z, x), doc: 8 (over y, core).
Axes of the slice: x: 4, y: 4, z: 4, core: 2. Of those that a mesh axis runs over, the one named last changes fastest.
Arguments:
- docs: bfloat16 [1048576, 768], P(('hst', 'doc')), may hold values from -400 to 400, as said below
- w_in: bfloat16 [768, 256], replicated, may hold values from -0.21875 to 0.21875
- w_out: bfloat16 [256, 64], replicated, may hold values from -0.375 to 0.375
- doc_host: int32 [1048576], P(('hst', 'doc')), may hold values from 0 to 2047
- tiles: bfloat16 [8192, 128, 128], P(('hst', 'doc')), may hold values from 0 to 10, as said below
- dst_block: int32 [8192], P(('hst', 'doc')), may hold values from 0 to 15
- src_block: int32 [8192], P(('hst', 'doc')), may hold values from 0 to 255
- tile_count: int32 [128], P(('hst', 'doc')), may hold values from 1 to 64, as said below
- teleport: int32 [32768], P('hst'), may hold values 0 or 1
Outputs:
- scores: float32 [32768, 64], P(('hst', 'doc'))
Inputs may be any that keep to these rules, and one draw needn't show every extreme that they name: `docs`: embeddings stay in the stated range. `tiles`: link weights are nonnegative. `tile_count`: some device uses all 64 slots.
All inputs are finite; a program needn't handle non-finite values. No bound on the sum of `teleport` on one device may be relied on, other than what follows from the above.
Results may differ from a plain program's by a relative error of at most 0.00066.
Values may be sent and summed in bfloat16 or wider, within the bound.
A program may use at most 128 MiB of HBM per device.

v0:
```python
import jax
import jax.numpy as jnp
from jax import lax
from jax.sharding import PartitionSpec as P

HOPS = 3


def body(docs, w_in, w_out, doc_host, tiles, dst_block, src_block, tile_count, teleport):
    host_dev = teleport.shape[0]
    block = tiles.shape[1]
    topics = w_out.shape[1]
    slots = tiles.shape[0]
    hosts_all = host_dev * lax.axis_size("hst")
    nblocks = hosts_all // block
    hidden = jax.nn.gelu(
        jnp.dot(docs, w_in, preferred_element_type=jnp.float32), approximate=True
    ).astype(jnp.bfloat16)
    probs = jax.nn.softmax(jnp.dot(hidden, w_out, preferred_element_type=jnp.float32), axis=-1)
    local_topic = jax.ops.segment_sum(probs, doc_host, num_segments=host_dev)
    used = (jnp.arange(slots) < tile_count[0]).astype(jnp.float32)
    colsum = jnp.sum(tiles, axis=1, dtype=jnp.float32)
    src_onehot = (src_block[:, None] == jnp.arange(nblocks)[None, :]).astype(jnp.float32) * used[
        :, None
    ]
    degree_blocks = jnp.dot(src_onehot.T, colsum, precision=lax.Precision.HIGHEST)
    degree = lax.psum(degree_blocks, ("hst", "doc")).reshape(hosts_all)
    own_degree = lax.dynamic_slice_in_dim(degree, lax.axis_index("hst") * host_dev, host_dev)
    inverse = 1.0 / jnp.maximum(own_degree, 1.0)
    dst_onehot = (dst_block[:, None] == jnp.arange(host_dev // block)[None, :]).astype(
        jnp.float32
    ) * used[:, None]
    member = teleport.astype(jnp.float32)
    rows = host_dev // lax.axis_size("doc")
    host_topic = lax.psum(local_topic, "doc")
    mass = lax.psum(jnp.sum(member[:, None] * host_topic, axis=0), "hst")
    tele = member[:, None] * host_topic / mass
    state = tele
    for hop in range(HOPS):
        sent = (state * inverse[:, None]).astype(jnp.bfloat16)
        full = lax.all_gather(sent, "hst", axis=0, tiled=True)
        slabs = full.reshape(nblocks, block, topics)[src_block]
        prod = jnp.einsum("kij,kjt->kit", tiles, slabs, preferred_element_type=jnp.float32)
        gathered = jnp.einsum("kb,kit->bit", dst_onehot, prod, precision=lax.Precision.HIGHEST)
        inflow = lax.psum(gathered.reshape(host_dev, topics), "doc")
        state = 0.85 * inflow + 0.15 * tele
    result = lax.dynamic_slice_in_dim(state, lax.axis_index("doc") * rows, rows)
    return hosts_all * result


def solution(mesh):
    placed = (
        P(("hst", "doc"), None),
        P(),
        P(),
        P(("hst", "doc")),
        P(("hst", "doc"), None, None),
        P(("hst", "doc")),
        P(("hst", "doc")),
        P(("hst", "doc")),
        P("hst"),
    )
    return jax.shard_map(
        body, mesh=mesh, in_specs=placed, out_specs=P(("hst", "doc"), None), check_vma=False
    )
```

profile of v0, /device:TPU:0, one launch (start us, length us, event | category | flops | bytes accessed | tf_op | source)
XLA Modules:
  0.0 640.4 jit_solution(17008999515403632906)
XLA Ops:
  7.3 2.1 convert_reduce_fusion
  9.4 1.8 convolution_bitcast_fusion
  11.2 8.6 %fusion.48 = (f32[8192]{0:T(1024)S(1)}, f32[8192,64]{0,1:T(8,128)S(1)}) fusion(bf16[256,64]{0,1:T(8,128)(2,1)} %param.11, bf16[8192,768]{1,0:T(8,128)(2,1)} %param.9, bf16[768,256]{1,0:T(8,128)(2,1)S(1)} %copy-done), kind=kOutput, calls=%fused_computation.78 | convolution fusion | flops 3509051392 | bytes 15138816 | tf_op jit(solution)/shard_map/dot_general | solution.py:19
  19.9 1.3 copy-done.2
  21.6 1.9 fusion.16
  23.5 2.7 copy.18
  26.2 44.5 %scatter_custom_fusion = f32[2048,64]{1,0:T(8,128)S(1)} fusion(s32[8192]{0:T(1024)} %param.12, f32[8192,64]{1,0:T(8,128)} %copy.18, f32[]{:T(128)} %constant.16.clone.1), kind=kCustom, calls=%fused_computation.37 | custom fusion | flops 524288 | bytes 524800 | tf_op jit(solution)/shard_map/scatter-add | solution.py:20
  72.0 82.8 %all-reduce.8.cloned.1.call-done = f32[32768]{0:T(1024)} async-done(((f32[32768]{0:T(1024)}), f32[32768]{0:T(1024)}) %all-reduce.8.cloned.1.call-update) | async-done | bytes 131088 | tf_op jit(solution)/shard_map/psum | solution.py:27
  155.5 59.7 %all-reduce.6.cloned.1.call-done = f32[2048,64]{0,1:T(8,128)} async-done(((f32[2048,64]{0,1:T(8,128)}), f32[2048,64]{0,1:T(8,128)}) %all-reduce.6.cloned.1.call-update) | async-done | bytes 524304 | tf_op jit(solution)/shard_map/psum | solution.py:35
  216.4 40.5 %psum.43 = f32[64]{0:T(128)S(1)} all-reduce(f32[64]{0:T(128)S(1)} %multiply_reduce_fusion), channel_id=1, replica_groups=mesh['hst'=16,'doc'=8] {'hst'}, use_global_device_ids=true, to_apply=%region_5.0 | all-reduce | flops 64 | bytes 512 | tf_op jit(solution)/shard_map/psum | solution.py:36
  256.9 1.9 multiply_convert_fusion.2
  259.7 44.7 %all-gather.4.cloned.1.call-done = bf16[32768,64]{0,1:T(8,128)(2,1)} async-done(((bf16[2048,64]{0,1:T(8,128)(2,1)}), bf16[32768,64]{0,1:T(8,128)(2,1)}) %all-gather.4.cloned.1.call-update) | async-done | bytes 4194320 | tf_op jit(solution)/shard_map/all_gather | solution.py:41
  304.4 5.4 copy_bitcast_fusion.2
  309.8 3.2 gather_fusion
  313.0 1.5 convolution_bitcast_fusion.3
  314.6 2.2 fusion.14
  317.8 60.4 %all-reduce.10.cloned.1.call-done = f32[2048,64]{0,1:T(8,128)} async-done(((f32[2048,64]{0,1:T(8,128)}), f32[2048,64]{0,1:T(8,128)}) %all-reduce.10.cloned.1.call-update) | async-done | bytes 524304 | tf_op jit(solution)/shard_map/psum | solution.py:45
  378.3 2.2 multiply_convert_fusion.1
  380.6 51.0 %all-gather.6.cloned.1.call-done = bf16[32768,64]{0,1:T(8,128)(2,1)} async-done(((bf16[2048,64]{0,1:T(8,128)(2,1)}), bf16[32768,64]{0,1:T(8,128)(2,1)}) %all-gather.6.cloned.1.call-update) | async-done | bytes 4194320 | tf_op jit(solution)/shard_map/all_gather | solution.py:41
  431.6 5.4 copy_bitcast_fusion.1
  436.9 3.1 gather_fusion.1
  440.0 1.5 convolution_bitcast_fusion.2
  441.6 2.2 fusion.12
  444.8 60.4 %all-reduce.12.cloned.1.call-done = f32[2048,64]{0,1:T(8,128)} async-done(((f32[2048,64]{0,1:T(8,128)}), f32[2048,64]{0,1:T(8,128)}) %all-reduce.12.cloned.1.call-update) | async-done | bytes 524304 | tf_op jit(solution)/shard_map/psum | solution.py:45
  505.3 1.8 multiply_convert_fusion
  507.4 51.0 %all-gather.8.cloned.1.call-done = bf16[32768,64]{0,1:T(8,128)(2,1)} async-done(((bf16[2048,64]{0,1:T(8,128)(2,1)}), bf16[32768,64]{0,1:T(8,128)(2,1)}) %all-gather.8.cloned.1.call-update) | async-done | bytes 4194320 | tf_op jit(solution)/shard_map/all_gather | solution.py:41
  558.4 5.4 copy_bitcast_fusion
  563.7 3.1 gather_fusion.2
  566.8 1.5 convolution_bitcast_fusion.1
  568.3 2.2 fusion.10
  571.6 60.5 %all-reduce.14.cloned.1.call-done = f32[2048,64]{0,1:T(8,128)} async-done(((f32[2048,64]{0,1:T(8,128)}), f32[2048,64]{0,1:T(8,128)}) %all-reduce.14.cloned.1.call-update) | async-done | bytes 524304 | tf_op jit(solution)/shard_map/psum | solution.py:45
  632.0 1.5 fusion.20
  (54 shorter events, 7.7 us)
Async XLA Ops:
  6.5 4.7 copy-start
  6.5 148.3 %all-reduce.8.cloned.1.call-start = ((), (), s32[]{:S(2)}) async-start(), calls=%async_computation.1 | async-start | bytes 262144 | tf_op jit(solution)/shard_map/psum | solution.py:27
  7.3 2.1 copy-start.5
  11.2 204.0 %all-reduce.6.cloned.1.call-start = ((), (), s32[]{:S(2)}) async-start(), calls=%async_computation | async-start | bytes 1048576 | tf_op jit(solution)/shard_map/psum | solution.py:35
  19.9 1.3 copy-start.2
  23.5 48.5 %copy-start.8 = (s32[2048]{0:T(1024)S(1)}, s32[2048]{0:T(1024)}, u32[]{:S(2)}) copy-start(s32[2048]{0:T(1024)} %param.17) | copy-start | bytes 24580
  23.5 235.5 %copy-start.13 = (s32[64]{0:T(128)S(1)}, s32[64]{0:T(128)}, u32[]{:S(2)}) copy-start(s32[64]{0:T(128)} %param.15) | copy-start | bytes 772
  71.9 232.4 %all-gather.4.cloned.1.call-start = ((), (), s32[]{:S(2)}) async-start(), calls=%async_computation.2 | async-start | bytes 4456448 | tf_op jit(solution)/shard_map/all_gather | solution.py:41
  256.9 47.5 %copy-start.11 = (f32[64]{0:T(128)}, f32[64]{0:T(128)S(1)}, u32[]{:S(2)}) copy-start(f32[64]{0:T(128)S(1)} %psum.43) | copy-start | bytes 772
  258.8 119.5 %all-reduce.10.cloned.1.call-start = ((), (), s32[]{:S(2)}) async-start(), calls=%async_computation.3 | async-start | bytes 1048576 | tf_op jit(solution)/shard_map/psum | solution.py:45
  309.8 3.2 copy-start.1
  313.0 1.6 copy-start.6
  313.0 1.6 copy-start.9
  314.6 63.7 %copy-start.3 = (f32[2048,64]{0,1:T(8,128)S(1)}, f32[2048,64]{0,1:T(8,128)}, u32[]{:S(2)}) copy-start(f32[2048,64]{0,1:T(8,128)} %all-reduce.6.cloned.1.call-done) | copy-start | bytes 1572868
  314.6 63.7 %copy-start.12 = (f32[64]{0:T(128)S(1)}, f32[64]{0:T(128)}, u32[]{:S(2)}) copy-start(f32[64]{0:T(128)} %copy-done.11) | copy-start | bytes 772
  317.8 113.8 %all-gather.6.cloned.1.call-start = ((), (), s32[]{:S(2)}) async-start(), calls=%async_computation.4 | async-start | bytes 4456448 | tf_op jit(solution)/shard_map/all_gather | solution.py:41
  380.5 124.8 %all-reduce.12.cloned.1.call-start = ((), (), s32[]{:S(2)}) async-start(), calls=%async_computation.5 | async-start | bytes 1048576 | tf_op jit(solution)/shard_map/psum | solution.py:45
  436.9 4.6 copy-start.7
  436.9 4.6 copy-start.10
  441.6 63.7 %copy-start.4 = (f32[2048,64]{0,1:T(8,128)S(1)}, f32[2048,64]{0,1:T(8,128)}, u32[]{:S(2)}) copy-start(f32[2048,64]{0,1:T(8,128)} %get-tuple-element.6) | copy-start | bytes 1572868
  444.8 113.6 %all-gather.8.cloned.1.call-start = ((), (), s32[]{:S(2)}) async-start(), calls=%async_computation.6 | async-start | bytes 4456448 | tf_op jit(solution)/shard_map/all_gather | solution.py:41
  507.1 124.9 %all-reduce.14.cloned.1.call-start = ((), (), s32[]{:S(2)}) async-start(), calls=%async_computation.7 | async-start | bytes 1048576 | tf_op jit(solution)/shard_map/psum | solution.py:45
Sparse Core Ops, SparseCore 0:
  12.1 142.6 all-reduce.7
  157.2 57.9 all-reduce.5
  258.9 45.3 all-gather.3
  317.9 60.3 all-reduce.9
  380.6 50.8 all-gather.5
  444.9 60.3 all-reduce.11
  507.4 50.8 all-gather.7
  571.7 60.3 all-reduce.13
where the time goes:
time: 641 us; the launch traced here: 640 us
  waiting for transfers between devices  471 us (73%)
  other arithmetic  58.8 us (9%)
  blocking collectives  40.5 us (6%)
  local copies, waits for them, and re-layouts  33.6 us (5%)
  matrix products  21.7 us (3%)
  between operations  14.4 us (2%)
    psum x3, waiting for transfers between devices, body(): inflow = lax.psum(gathered.reshape(host_dev, topics), 'doc')  181 us
    all_gather x3, waiting for transfers between devices, body(): full = lax.all_gather(sent, 'hst', axis=0, tiled=True)  147 us
    psum x1, waiting for transfers between devices, body(): degree = lax.psum(degree_blocks, ('hst', 'doc')).reshape(hosts_all)  82.8 us
    psum x1, waiting for transfers between devices, body(): host_topic = lax.psum(local_topic, 'doc')  59.7 us
    scatter-add x1, other arithmetic, body(): local_topic = jax.ops.segment_sum(probs, doc_host, num_segments=host_dev)  44.5 us
    psum x1, blocking collectives, body(): mass = lax.psum(jnp.sum(member[:, None] * host_topic, axis=0), 'hst')  40.5 us
    reshape x3, local copies, waits for them, and re-layouts, body(): slabs = full.reshape(nblocks, block, topics)[src_block]  16.1 us
  transfers between devices with their start and end apart: 8, of which 8 were waited for; matrix products, arithmetic and copies ran while one was open for 9% of the time, Pallas kernels for 0%

commit v1 on v0

--- a/solution.py
+++ b/solution.py
@@ -38,7 +38,9 @@
     state = tele
     for hop in range(HOPS):
         sent = (state * inverse[:, None]).astype(jnp.bfloat16)
-        full = lax.all_gather(sent, "hst", axis=0, tiled=True)
+        full = jnp.concatenate(
+            lax.all_to_all(jnp.stack([sent] * lax.axis_size("hst")), "hst", 0, 0), axis=0
+        )
         slabs = full.reshape(nblocks, block, topics)[src_block]
         prod = jnp.einsum("kij,kjt->kit", tiles, slabs, preferred_element_type=jnp.float32)
         gathered = jnp.einsum("kb,kit->bit", dst_onehot, prod, precision=lax.Precision.HIGHEST)

time: 641 us -> 701 us (1.094)
  blocking collectives: 40.5 us -> 153 us
  waiting for transfers between devices: 471 us -> 365 us
  local copies, waits for them, and re-layouts: 33.6 us -> 78.4 us
    all_gather x3 -> x0, waiting for transfers between devices: 147 us -> none  [body(): full = lax.all_gather(sent, 'hst', axis=0, tiled=True)]
    all_to_all x0 -> x2, blocking collectives: none -> 112 us  [body(): lax.all_to_all(jnp.stack([sent] * lax.axis_size('hst')), 'hst', 0, 0)]
    all_to_all x0 -> x1, waiting for transfers between devices: none -> 46.9 us  [body(): lax.all_to_all(jnp.stack([sent] * lax.axis_size('hst')), 'hst', 0, 0)]
    another operation x0 -> x9, local copies, waits for them, and re-layouts: none -> 46.3 us  [the longest x6 42.8 us: body(): slabs = full.reshape(nblocks, block, topics)[src_block]]
    reshape x3 -> x0, local copies, waits for them, and re-layouts: 16.1 us -> none  [body(): slabs = full.reshape(nblocks, block, topics)[src_block]]
    all_to_all x0 -> x3, local copies, waits for them, and re-layouts: none -> 15 us  [body(): lax.all_to_all(jnp.stack([sent] * lax.axis_size('hst')), 'hst', 0, 0)]
  transfers between devices with their start and end apart: 8 -> 6, of which waited for: 8 -> 6; matrix products, arithmetic and copies ran while one was open for 9% -> 9% of each run, Pallas kernels for 0% -> 0%
where the time goes in v1:
time: 701 us; the launch traced here: 694 us
  waiting for transfers between devices  365 us (52%)
  blocking collectives  153 us (22%)
  local copies, waits for them, and re-layouts  78.4 us (11%)
  other arithmetic  56.6 us (8%)
  matrix products  21 us (3%)
  between operations  14.3 us (2%)
    psum x3, waiting for transfers between devices, body(): inflow = lax.psum(gathered.reshape(host_dev, topics), 'doc')  175 us
    all_to_all x2, blocking collectives, body(): lax.all_to_all(jnp.stack([sent] * lax.axis_size('hst')), 'hst', 0, 0)  112 us
    psum x1, waiting for transfers between devices, body(): degree = lax.psum(degree_blocks, ('hst', 'doc')).reshape(hosts_all)  83.6 us
    psum x1, waiting for transfers between devices, body(): host_topic = lax.psum(local_topic, 'doc')  59.7 us
    all_to_all x1, waiting for transfers between devices, body(): lax.all_to_all(jnp.stack([sent] * lax.axis_size('hst')), 'hst', 0, 0)  46.9 us
    scatter-add x1, other arithmetic, body(): local_topic = jax.ops.segment_sum(probs, doc_host, num_segments=host_dev)  44.5 us
    another operation x6, local copies, waits for them, and re-layouts, body(): slabs = full.reshape(nblocks, block, topics)[src_block]  42.8 us
    psum x1, blocking collectives, body(): mass = lax.psum(jnp.sum(member[:, None] * host_topic, axis=0), 'hst')  40.5 us
  transfers between devices with their start and end apart: 6, of which 6 were waited for; matrix products, arithmetic and copies ran while one was open for 9% of the time, Pallas kernels for 0%

profile of v1, /device:TPU:0, one launch (start us, length us, event | category | flops | bytes accessed | tf_op | source)
XLA Modules:
  0.0 693.7 jit_solution(10600079217067721954)
XLA Ops:
  7.3 2.1 convert_reduce_fusion
  10.6 8.6 %fusion.48 = (f32[8192]{0:T(1024)S(1)}, f32[8192,64]{0,1:T(8,128)S(1)}) fusion(bf16[256,64]{0,1:T(8,128)(2,1)S(1)} %copy-done.9, bf16[8192,768]{1,0:T(8,128)(2,1)} %param.9, bf16[768,256]{1,0:T(8,128)(2,1)S(1)} %copy-done), kind=kOutput, calls=%fused_computation.75 | convolution fusion | flops 3509051392 | bytes 15138816 | tf_op jit(solution)/shard_map/dot_general | solution.py:19
  20.9 1.9 fusion.16
  22.8 2.7 copy.46
  25.5 44.5 %scatter_custom_fusion = f32[2048,64]{1,0:T(8,128)S(1)} fusion(s32[8192]{0:T(1024)} %param.12, f32[8192,64]{1,0:T(8,128)} %copy.46, f32[]{:T(128)} %constant.16.clone.1), kind=kCustom, calls=%fused_computation.34 | custom fusion | flops 524288 | bytes 524800 | tf_op jit(solution)/shard_map/scatter-add | solution.py:20
  71.2 83.6 %all-reduce.8.cloned.1.call-done = f32[32768]{0:T(1024)} async-done(((f32[32768]{0:T(1024)}), f32[32768]{0:T(1024)}) %all-reduce.8.cloned.1.call-update) | async-done | bytes 131088 | tf_op jit(solution)/shard_map/psum | solution.py:27
  155.5 59.7 %all-reduce.6.cloned.1.call-done = f32[2048,64]{0,1:T(8,128)} async-done(((f32[2048,64]{0,1:T(8,128)}), f32[2048,64]{0,1:T(8,128)}) %all-reduce.6.cloned.1.call-update) | async-done | bytes 524304 | tf_op jit(solution)/shard_map/psum | solution.py:35
  216.4 40.5 %psum.43 = f32[64]{0:T(128)S(1)} all-reduce(f32[64]{0:T(128)S(1)} %multiply_reduce_fusion), channel_id=1, replica_groups=mesh['hst'=16,'doc'=8] {'hst'}, use_global_device_ids=true, to_apply=%region_5.0 | all-reduce | flops 64 | bytes 512 | tf_op jit(solution)/shard_map/psum | solution.py:36
  258.1 2.5 stack.6
  260.6 4.5 all-to-all-start
  265.7 46.9 %all-to-all-done = bf16[16,2048,64]{1,2,0:T(8,128)(2,1)} async-done(((bf16[16,2048,64]{1,2,0:T(8,128)(2,1)}), bf16[16,2048,64]{1,2,0:T(8,128)(2,1)}, u32[]{:S(2)}, u32[]{:S(2)}) %all-to-all-start) | async-done | bytes 4194336 | tf_op jit(solution)/shard_map/all_to_all | solution.py:42
  312.6 6.5 copy.48
  319.0 7.4 %reshape_reshape.9 = bf16[256,128,64]{1,0,2:T(8,128)(2,1)} reshape(bf16[16,2048,64]{1,0,2:T(8,128)(2,1)} %copy.48) | data formatting | bytes 8388608 | tf_op jit(solution)/shard_map/reshape;reshape | solution.py:44
  326.4 6.9 copy.49
  333.3 3.1 gather_fusion
  338.0 2.2 fusion.14
  341.2 57.3 %all-reduce.10.cloned.1.call-done = f32[2048,64]{0,1:T(8,128)} async-done(((f32[2048,64]{0,1:T(8,128)}), f32[2048,64]{0,1:T(8,128)}) %all-reduce.10.cloned.1.call-update) | async-done | bytes 524304 | tf_op jit(solution)/shard_map/psum | solution.py:47
  398.5 2.1 multiply_convert_fusion.1
  401.1 56.1 %all_to_all.15 = bf16[16,2048,64]{1,2,0:T(8,128)(2,1)S(1)} all-to-all(bf16[16,2048,64]{1,2,0:T(8,128)(2,1)S(1)} %stack.7), channel_id=1, replica_groups=mesh['hst'=16,'doc'=8] {'hst'}, dimensions={0} | all-to-all | bytes 8388608 | tf_op jit(solution)/shard_map/all_to_all | solution.py:42
  457.2 4.3 copy.51
  461.5 7.4 %reshape_reshape.10 = bf16[256,128,64]{1,0,2:T(8,128)(2,1)} reshape(bf16[16,2048,64]{1,0,2:T(8,128)(2,1)} %copy.51) | data formatting | bytes 8388608 | tf_op jit(solution)/shard_map/reshape;reshape | solution.py:44
  468.9 6.9 copy.52
  475.8 2.9 gather_fusion.1
  480.2 2.2 fusion.12
  483.5 58.9 %all-reduce.12.cloned.1.call-done = f32[2048,64]{0,1:T(8,128)} async-done(((f32[2048,64]{0,1:T(8,128)}), f32[2048,64]{0,1:T(8,128)}) %all-reduce.12.cloned.1.call-update) | async-done | bytes 524304 | tf_op jit(solution)/shard_map/psum | solution.py:47
  544.1 56.1 %all_to_all.16 = bf16[16,2048,64]{1,2,0:T(8,128)(2,1)S(1)} all-to-all(bf16[16,2048,64]{1,2,0:T(8,128)(2,1)S(1)} %stack.8), channel_id=1, replica_groups=mesh['hst'=16,'doc'=8] {'hst'}, dimensions={0} | all-to-all | bytes 8388608 | tf_op jit(solution)/shard_map/all_to_all | solution.py:42
  600.2 4.3 copy.54
  604.5 7.4 %reshape_reshape.11 = bf16[256,128,64]{1,0,2:T(8,128)(2,1)} reshape(bf16[16,2048,64]{1,0,2:T(8,128)(2,1)} %copy.54) | data formatting | bytes 8388608 | tf_op jit(solution)/shard_map/reshape;reshape | solution.py:44
  611.9 6.9 copy.55
  618.7 2.9 gather_fusion.2
  623.2 2.2 fusion.10
  626.5 58.9 %all-reduce.14.cloned.1.call-done = f32[2048,64]{0,1:T(8,128)} async-done(((f32[2048,64]{0,1:T(8,128)}), f32[2048,64]{0,1:T(8,128)}) %all-reduce.14.cloned.1.call-update) | async-done | bytes 524304 | tf_op jit(solution)/shard_map/psum | solution.py:47
  (50 shorter events, 18.9 us)
Async XLA Ops:
  6.5 4.0 copy-start
  6.5 2.8 copy-start.8
  6.5 4.0 copy-start.9
  6.5 148.3 %all-reduce.8.cloned.1.call-start = ((), (), s32[]{:S(2)}) async-start(), calls=%async_computation.4 | async-start | bytes 262144 | tf_op jit(solution)/shard_map/psum | solution.py:27
  10.5 204.7 %all-reduce.6.cloned.1.call-start = ((), (), s32[]{:S(2)}) async-start(), calls=%async_computation.3 | async-start | bytes 1048576 | tf_op jit(solution)/shard_map/psum | solution.py:35
  19.2 1.4 copy-start.3
  25.5 45.7 %copy-start.6 = (s32[2048]{0:T(1024)S(1)}, s32[2048]{0:T(1024)}, u32[]{:S(2)}) copy-start(s32[2048]{0:T(1024)} %param.17) | copy-start | bytes 24580
  260.6 52.0 %all-to-all-start = ((bf16[16,2048,64]{1,2,0:T(8,128)(2,1)}), bf16[16,2048,64]{1,2,0:T(8,128)(2,1)}, u32[]{:S(2)}, u32[]{:S(2)}) async-start(bf16[16,2048,64]{1,2,0:T(8,128)(2,1)} %stack.6), calls=%async_computation | async-start | bytes 8388608 | tf_op jit(solution)/shard_map/all_to_all | solution.py:42
  265.1 133.4 %all-reduce.10.cloned.1.call-start = ((), (), s32[]{:S(2)}) async-start(), calls=%async_computation.5 | async-start | bytes 1048576 | tf_op jit(solution)/shard_map/psum | solution.py:47
  333.3 3.1 copy-start.2
  336.4 1.6 copy-start.7
  338.0 60.6 %copy-start.4 = (f32[2048,64]{0,1:T(8,128)S(1)}, f32[2048,64]{0,1:T(8,128)}, u32[]{:S(2)}) copy-start(f32[2048,64]{0,1:T(8,128)} %all-reduce.6.cloned.1.call-done) | copy-start | bytes 1572868
  341.2 201.2 %all-reduce.12.cloned.1.call-start = ((), (), s32[]{:S(2)}) async-start(), calls=%async_computation.6 | async-start | bytes 1048576 | tf_op jit(solution)/shard_map/psum | solution.py:47
  480.2 62.2 %copy-start.5 = (f32[2048,64]{0,1:T(8,128)S(1)}, f32[2048,64]{0,1:T(8,128)}, u32[]{:S(2)}) copy-start(f32[2048,64]{0,1:T(8,128)} %get-tuple-element.6) | copy-start | bytes 1572868
  483.5 201.9 %all-reduce.14.cloned.1.call-start = ((), (), s32[]{:S(2)}) async-start(), calls=%async_computation.7 | async-start | bytes 1048576 | tf_op jit(solution)/shard_map/psum | solution.py:47
  621.7 65.2 %copy-start.1 = (bf16[768,256]{1,0:T(8,128)(2,1)S(1)}, bf16[768,256]{1,0:T(8,128)(2,1)}, u32[]{:S(2)}) copy-start(bf16[768,256]{1,0:T(8,128)(2,1)} %param.10) | copy-start | bytes 1179652
Sparse Core Ops, SparseCore 0:
  12.1 142.6 all-reduce.7
  157.2 57.9 all-reduce.5
  341.3 57.1 all-reduce.9
  483.6 58.7 all-reduce.11
  626.6 58.7 all-reduce.13
